TPU v7x, 256 devices: a whole 4x4x8 slice. The times are simulated.
256 devices in a mesh: row: 4 (over y), col: 16 (over z, core), layer: 4 (over x).
Axes of the slice: x: 4, y: 4, z: 8, core: 2. Of those that a mesh axis runs over, the one named last changes fastest.
Arguments:
- density: float32 [4096, 4096], P('row', 'col'), may hold values from -1 to 1, as said below
- pattern: int32 [64, 64], replicated, may hold values from 0 to 1, as said below
Outputs:
- purified: float32 [4096, 4096], P('row', 'col')
- traces: float32 [2], replicated
Inputs may be any that keep to these rules, and one draw needn't show every extreme that they name: pattern is symmetric and is 1 on the block diagonal and next to it. density is symmetric and zero outside the blocks that pattern keeps.
All inputs are finite; a program needn't handle non-finite values.
Results may differ from a plain program's by a relative error of at most 0.0003.
Values sent between devices are 32-bit elements; how exact they have to be, the bound alone decides.
No kernel may reach another device: no remote copies, remote signals or barrier semaphores. Data moves between devices by JAX's collectives and lax.ppermute only.
A program may use at most 64 MiB of HBM per device.

v0:
```python
import jax
import jax.numpy as jnp
from jax import lax
from jax.sharding import PartitionSpec as P

BS = 64
STEPS = 2
HIGHEST = lax.Precision.HIGHEST


def pick_columns(tile, layer_index, unit_width, layers):
    tile_rows, tile_cols = tile.shape
    shaped = tile.reshape(tile_rows, tile_cols // (layers * unit_width), layers, unit_width)
    picked = lax.dynamic_index_in_dim(shaped, layer_index, 2, keepdims=False)
    return picked.reshape(tile_rows, tile_cols // layers)


def pick_rows(tile, layer_index, unit_width, layers):
    tile_rows, tile_cols = tile.shape
    shaped = tile.reshape(tile_rows // (layers * unit_width), layers, unit_width, tile_cols)
    picked = lax.dynamic_index_in_dim(shaped, layer_index, 1, keepdims=False)
    return picked.reshape(tile_rows // layers, tile_cols)


def reduce_layers(layer_term):
    summed = lax.psum(layer_term, "layer")
    return summed


def right_panel(right, layer_index, unit_width, layers):
    return lax.all_gather(
        pick_rows(right, layer_index, unit_width, layers), "row", axis=0, tiled=True
    )


def folded_product(left, right, layer_index, unit_width, layers, occupied):
    tall_panel = right_panel(right, layer_index, unit_width, layers)
    layer_term = jnp.dot(
        lax.all_gather(
            pick_columns(left, layer_index, unit_width, layers), "col", axis=1, tiled=True
        ),
        tall_panel,
        precision=HIGHEST,
        preferred_element_type=jnp.float32,
    )
    summed = reduce_layers(layer_term)
    return jnp.where(occupied, summed, jnp.zeros_like(summed))


def body(density, pattern):
    tile_rows, tile_cols = density.shape
    layers = lax.axis_size("layer")
    unit_width = tile_cols // (lax.axis_size("row") * layers)
    layer_index = lax.axis_index("layer")
    row_ids = lax.axis_index("row") * tile_rows + jnp.arange(tile_rows, dtype=jnp.int32)
    col_ids = lax.axis_index("col") * tile_cols + jnp.arange(tile_cols, dtype=jnp.int32)
    blocks = jnp.arange(pattern.shape[0], dtype=jnp.int32)
    row_onehot = (row_ids[:, None] // BS == blocks[None, :]).astype(jnp.bfloat16)
    col_onehot = (blocks[:, None] == col_ids[None, :] // BS).astype(jnp.bfloat16)
    row_pattern = jnp.dot(
        row_onehot, pattern.astype(jnp.bfloat16), preferred_element_type=jnp.float32
    )
    occupied = (
        jnp.dot(row_pattern.astype(jnp.bfloat16), col_onehot, preferred_element_type=jnp.float32)
        > 0.5
    )
    on_diag = row_ids[:, None] == col_ids[None, :]
    current = density
    trace_list = []
    for iteration in range(STEPS):
        square = folded_product(current, current, layer_index, unit_width, layers, occupied)
        cube_term = folded_product(current, square, layer_index, unit_width, layers, occupied)
        current = 3.0 * square - 2.0 * cube_term
        diag_part = jnp.sum(jnp.where(on_diag, current, jnp.zeros_like(current)))
        trace_list.append(lax.psum(diag_part, ("row", "col")))
    stacked = jnp.stack(trace_list)
    return (current, stacked)


def solution(mesh):
    placed = (P("row", "col"), P())
    return jax.shard_map(
        body, mesh=mesh, in_specs=placed, out_specs=(P("row", "col"), P()), check_vma=False
    )
```

profile of v0, /device:TPU:2, one launch (start us, length us, event | category | flops | bytes accessed | tf_op | source)
XLA Modules:
  0.0 601.4 jit_solution(12206215405275679510)
XLA Ops:
  7.2 0.0 all-gather.9.cloned.1.call-start
  7.2 1.7 constant_dynamic-slice_fusion.4
  8.9 0.0 all-gather.9.cloned.1.call-update
  8.9 0.0 all-gather.7.cloned.1.call-start
  9.0 1.6 copy.4
  10.6 0.7 constant_dynamic-slice_fusion.5
  11.3 0.0 all-gather.7.cloned.1.call-update
  11.3 0.0 all-reduce.6.cloned.1.call-start
  11.4 28.0 %all-gather.9.cloned.1.call-done = f32[1024,256]{1,0:T(8,128)} async-done(((f32[256,256]{1,0:T(8,128)}), f32[1024,256]{1,0:T(8,128)}) %all-gather.9.cloned.1.call-update) | async-done | bytes 1048592 | tf_op jit(solution)/shard_map/all_gather | solution.py:31
  39.3 44.9 %all-gather.7.cloned.1.call-done = f32[1024,1024]{0,1:T(8,128)} async-done(((f32[1024,64]{0,1:T(8,128)}), f32[1024,1024]{0,1:T(8,128)}) %all-gather.7.cloned.1.call-update) | async-done | bytes 4194320 | tf_op jit(solution)/shard_map/all_gather | solution.py:39
  84.2 10.1 %fusion.12 = f32[1024,256]{1,0:T(8,128)} fusion(f32[1024,1024]{0,1:T(8,128)} %all-gather.7.cloned.1.call-done, f32[1024,256]{1,0:T(8,128)} %all-gather.9.cloned.1.call-done), kind=kOutput, calls=%fused_computation.36 | convolution fusion | flops 3221225472 | bytes 6291456 | tf_op jit(solution)/shard_map/dot_general | solution.py:38
  94.3 0.0 all-reduce.6.cloned.1.call-update
  94.4 0.0 all-gather.11.cloned.1.call-start
  94.4 48.7 %all-reduce.6.cloned.1.call-done = f32[1024,256]{1,0:T(8,128)} async-done(((f32[1024,256]{1,0:T(8,128)}), f32[1024,256]{1,0:T(8,128)}) %all-reduce.6.cloned.1.call-update) | async-done | bytes 1048592 | tf_op jit(solution)/shard_map/psum | solution.py:26
  143.2 1.8 broadcast_select_fusion.1
  145.0 0.7 constant_dynamic-slice_fusion.3
  145.7 0.0 all-gather.11.cloned.1.call-update
  145.7 0.2 all-reduce.8.cloned.1.call-start
  146.0 28.2 %all-gather.11.cloned.1.call-done = f32[1024,256]{1,0:T(8,128)} async-done(((f32[256,256]{1,0:T(8,128)}), f32[1024,256]{1,0:T(8,128)}) %all-gather.11.cloned.1.call-update) | async-done | bytes 1048592 | tf_op jit(solution)/shard_map/all_gather | solution.py:31
  174.1 10.1 %fusion.13 = f32[1024,256]{1,0:T(8,128)} fusion(f32[1024,1024]{0,1:T(8,128)} %all-gather.7.cloned.1.call-done, f32[1024,256]{1,0:T(8,128)} %all-gather.11.cloned.1.call-done), kind=kOutput, calls=%fused_computation.37 | convolution fusion | flops 3221225472 | bytes 6291456 | tf_op jit(solution)/shard_map/dot_general | solution.py:38
  184.2 0.0 all-reduce.8.cloned.1.call-update
  184.3 0.0 all-gather.15.cloned.1.call-start
  184.3 50.6 %all-reduce.8.cloned.1.call-done = f32[1024,256]{1,0:T(8,128)} async-done(((f32[1024,256]{1,0:T(8,128)}), f32[1024,256]{1,0:T(8,128)}) %all-reduce.8.cloned.1.call-update) | async-done | bytes 1048592 | tf_op jit(solution)/shard_map/psum | solution.py:26
  234.9 1.5 multiply_subtract_fusion.1
  236.3 0.8 constant_dynamic-slice_fusion.1
  237.1 0.0 all-gather.15.cloned.1.call-update
  237.1 0.0 all-gather.13.cloned.1.call-start
  237.2 0.3 copy.5
  237.5 0.7 constant_dynamic-slice_fusion.2
  238.2 0.0 all-gather.13.cloned.1.call-update
  238.2 0.3 all-reduce.10.cloned.1.call-start
  238.5 27.0 %all-gather.15.cloned.1.call-done = f32[1024,256]{1,0:T(8,128)} async-done(((f32[256,256]{1,0:T(8,128)}), f32[1024,256]{1,0:T(8,128)}) %all-gather.15.cloned.1.call-update) | async-done | bytes 1048592 | tf_op jit(solution)/shard_map/all_gather | solution.py:31
  265.5 44.9 %all-gather.13.cloned.1.call-done = f32[1024,1024]{0,1:T(8,128)} async-done(((f32[1024,64]{0,1:T(8,128)}), f32[1024,1024]{0,1:T(8,128)}) %all-gather.13.cloned.1.call-update) | async-done | bytes 4194320 | tf_op jit(solution)/shard_map/all_gather | solution.py:39
  310.4 10.1 %fusion.14 = f32[1024,256]{1,0:T(8,128)} fusion(f32[1024,1024]{0,1:T(8,128)} %all-gather.13.cloned.1.call-done, f32[1024,256]{1,0:T(8,128)} %all-gather.15.cloned.1.call-done), kind=kOutput, calls=%fused_computation.38 | convolution fusion | flops 3221225472 | bytes 6291456 | tf_op jit(solution)/shard_map/dot_general | solution.py:38
  320.5 0.0 all-reduce.10.cloned.1.call-update
  320.5 0.0 all-gather.17.cloned.1.call-start
  320.5 48.8 %all-reduce.10.cloned.1.call-done = f32[1024,256]{1,0:T(8,128)} async-done(((f32[1024,256]{1,0:T(8,128)}), f32[1024,256]{1,0:T(8,128)}) %all-reduce.10.cloned.1.call-update) | async-done | bytes 1048592 | tf_op jit(solution)/shard_map/psum | solution.py:26
  369.3 1.3 broadcast_select_fusion
  370.7 0.7 constant_dynamic-slice_fusion
  371.4 0.0 all-gather.17.cloned.1.call-update
  371.4 0.3 all-reduce.12.cloned.1.call-start
  371.8 28.4 %all-gather.17.cloned.1.call-done = f32[1024,256]{1,0:T(8,128)} async-done(((f32[256,256]{1,0:T(8,128)}), f32[1024,256]{1,0:T(8,128)}) %all-gather.17.cloned.1.call-update) | async-done | bytes 1048592 | tf_op jit(solution)/shard_map/all_gather | solution.py:31
  400.1 10.1 %fusion.15 = f32[1024,256]{1,0:T(8,128)} fusion(f32[1024,1024]{0,1:T(8,128)} %all-gather.13.cloned.1.call-done, f32[1024,256]{1,0:T(8,128)} %all-gather.17.cloned.1.call-done), kind=kOutput, calls=%fused_computation.39 | convolution fusion | flops 3221225472 | bytes 6291456 | tf_op jit(solution)/shard_map/dot_general | solution.py:38
  410.2 0.0 all-reduce.12.cloned.1.call-update
  410.3 50.6 %all-reduce.12.cloned.1.call-done = f32[1024,256]{1,0:T(8,128)} async-done(((f32[1024,256]{1,0:T(8,128)}), f32[1024,256]{1,0:T(8,128)}) %all-reduce.12.cloned.1.call-update) | async-done | bytes 1048592 | tf_op jit(solution)/shard_map/psum | solution.py:26
  460.9 3.2 fusion
  464.1 128.6 %all-reduce = (f32[1]{0:T(128)}, f32[1]{0:T(128)}) all-reduce(f32[1]{0:T(128)} %bitcast.13, f32[1]{0:T(128)} %bitcast.12), channel_id=1, replica_groups=mesh['row'=4,'col'=16,'layer'=4] {'row','col'}, use_global_device_ids=true, to_apply=%region_7.8 | all-reduce | flops 2 | bytes 16 | tf_op jit(solution)/shard_map/psum | solution.py:75
  592.7 1.8 pad_maximum_fusion
  (10 shorter events, 0.1 us)
Async XLA Ops:
  7.2 32.2 %all-gather.9.cloned.1.call-start = ((), (), s32[]{:S(2)}) async-start(), calls=%async_computation.1 | async-start | bytes 1310720 | tf_op jit(solution)/shard_map/all_gather | solution.py:31
  8.9 75.3 %all-gather.7.cloned.1.call-start = ((), (), s32[]{:S(2)}) async-start(), calls=%async_computation | async-start | bytes 4456448 | tf_op jit(solution)/shard_map/all_gather | solution.py:39
  10.6 132.6 %copy-start.2 = (s32[64,64]{1,0:T(8,128)S(1)}, s32[64,64]{1,0:T(8,128)}, u32[]{:S(2)}) copy-start(s32[64,64]{1,0:T(8,128)} %param.3) | copy-start | bytes 49156
  11.3 131.9 %all-reduce.6.cloned.1.call-start = ((), (), s32[]{:S(2)}) async-start(), calls=%async_computation.2 | async-start | bytes 2097152 | tf_op jit(solution)/shard_map/psum | solution.py:26
  94.4 79.8 %all-gather.11.cloned.1.call-start = ((), (), s32[]{:S(2)}) async-start(), calls=%async_computation.3 | async-start | bytes 1310720 | tf_op jit(solution)/shard_map/all_gather | solution.py:31
  145.0 89.9 %copy-start.1 = (f32[1024,256]{1,0:T(8,128)S(1)}, f32[1024,256]{1,0:T(8,128)}, u32[]{:S(2)}) copy-start(f32[1024,256]{1,0:T(8,128)} %all-reduce.6.cloned.1.call-done) | copy-start | bytes 3145732
  145.7 89.1 %all-reduce.8.cloned.1.call-start = ((), (), s32[]{:S(2)}) async-start(), calls=%async_computation.4 | async-start | bytes 2097152 | tf_op jit(solution)/shard_map/psum | solution.py:26
  184.3 81.2 %all-gather.15.cloned.1.call-start = ((), (), s32[]{:S(2)}) async-start(), calls=%async_computation.6 | async-start | bytes 1310720 | tf_op jit(solution)/shard_map/all_gather | solution.py:31
  237.1 73.2 %all-gather.13.cloned.1.call-start = ((), (), s32[]{:S(2)}) async-start(), calls=%async_computation.5 | async-start | bytes 4456448 | tf_op jit(solution)/shard_map/all_gather | solution.py:39
  238.2 131.1 %all-reduce.10.cloned.1.call-start = ((), (), s32[]{:S(2)}) async-start(), calls=%async_computation.7 | async-start | bytes 2097152 | tf_op jit(solution)/shard_map/psum | solution.py:26
  320.5 79.6 %all-gather.17.cloned.1.call-start = ((), (), s32[]{:S(2)}) async-start(), calls=%async_computation.8 | async-start | bytes 1310720 | tf_op jit(solution)/shard_map/all_gather | solution.py:31
  370.7 90.2 %copy-start = (f32[1024,256]{1,0:T(8,128)S(1)}, f32[1024,256]{1,0:T(8,128)}, u32[]{:S(2)}) copy-start(f32[1024,256]{1,0:T(8,128)} %all-reduce.10.cloned.1.call-done) | copy-start | bytes 3145732
  371.4 89.4 %all-reduce.12.cloned.1.call-start = ((), (), s32[]{:S(2)}) async-start(), calls=%async_computation.9 | async-start | bytes 2097152 | tf_op jit(solution)/shard_map/psum | solution.py:26
Sparse Core Ops, SparseCore 0:
  9.8 29.4 all-gather.8
  41.7 42.4 all-gather.6
  94.5 48.6 all-reduce.5
  145.8 28.2 all-gather.10
  184.4 50.4 all-reduce.7
  237.2 28.2 all-gather.14
  267.9 42.4 all-gather.12
  320.6 48.6 all-reduce.9
  371.9 28.2 all-gather.16
  410.4 50.4 all-reduce.11
where the time goes:
time: 602 us; the launch traced here: 601 us
  waiting for transfers between devices  400 us (66%)
  blocking collectives  129 us (21%)
  matrix products  42.3 us (7%)
  between operations  14.3 us (2%)
  other arithmetic  7.89 us (1%)
  local copies, waits for them, and re-layouts  7.27 us (1%)
    psum x4, waiting for transfers between devices, reduce_layers(): summed = lax.psum(layer_term, 'layer')  199 us
    psum x1, blocking collectives, body(): trace_list.append(lax.psum(diag_part, ('row', 'col')))  129 us
    all_gather x4, waiting for transfers between devices, right_panel(): lax.all_gather(pick_rows(right, layer_index, unit_width, layers), 'row',...  111 us
    all_gather x2, waiting for transfers between devices, folded_product(): lax.all_gather(pick_columns(left, layer_index, unit_width, layers), 'col'...  89.7 us
    dot_general x4, matrix products, folded_product(): jnp.dot(lax.all_gather(pick_columns(left, layer_index, unit_width, layers...  40.5 us
  transfers between devices with their start and end apart: 10, of which 10 were waited for; matrix products, arithmetic and copies ran while one was open for 1% of the time, Pallas kernels for 0%

commit v1 on v0

--- a/solution.py
+++ b/solution.py
@@ -23,7 +23,7 @@
 
 
 def reduce_layers(layer_term):
-    summed = lax.psum(layer_term, "layer")
+    summed = jnp.sum(lax.all_gather(layer_term, "layer"), axis=0)
     return summed
 
 

time: 602 us -> 606 us (level)
  other arithmetic: 7.89 us -> 14.6 us
    all_gather x0 -> x4, waiting for transfers between devices: none -> 199 us  [reduce_layers(): summed = jnp.sum(lax.all_gather(layer_term, 'layer'), axis=0)]
    psum x4 -> x0, waiting for transfers between devices: 199 us -> none  [reduce_layers(): summed = lax.psum(layer_term, 'layer')]
    reduce_sum x0 -> x4, other arithmetic: none -> 10.4 us  [reduce_layers(): summed = jnp.sum(lax.all_gather(layer_term, 'layer'), axis=0)]
where the time goes in v1:
time: 606 us
  waiting for transfers between devices  398 us (66%)
  blocking collectives  130 us (21%)
  matrix products  41 us (7%)
  other arithmetic  14.6 us (2%)
  between operations  14.3 us (2%)
  local copies, waits for them, and re-layouts  7.25 us (1%)
    all_gather x4, waiting for transfers between devices, reduce_layers(): summed = jnp.sum(lax.all_gather(layer_term, 'layer'), axis=0)  199 us
    psum x1, blocking collectives, body(): trace_list.append(lax.psum(diag_part, ('row', 'col')))  130 us
    all_gather x4, waiting for transfers between devices, right_panel(): lax.all_gather(pick_rows(right, layer_index, unit_width, layers), 'row',...  109 us
    all_gather x2, waiting for transfers between devices, folded_product(): lax.all_gather(pick_columns(left, layer_index, unit_width, layers), 'col'...  89.7 us
    dot_general x4, matrix products, folded_product(): jnp.dot(lax.all_gather(pick_columns(left, layer_index, unit_width, layers...  40.5 us
  transfers between devices with their start and end apart: 10, of which 10 were waited for; matrix products, arithmetic and copies ran while one was open for 1% of the time, Pallas kernels for 0%

profile of v1, /device:TPU:2, one launch (start us, length us, event | category | flops | bytes accessed | tf_op | source)
XLA Modules:
  0.0 605.8 jit_solution(403896020922950800)
XLA Ops:
  7.2 0.0 all-gather.17.cloned.1.call-start
  7.2 1.7 constant_dynamic-slice_fusion.4
  8.9 0.0 all-gather.17.cloned.1.call-update
  8.9 0.0 all-gather.15.cloned.1.call-start
  9.0 1.6 copy.4
  10.5 0.7 constant_dynamic-slice_fusion.5
  11.3 0.0 all-gather.15.cloned.1.call-update
  11.3 0.0 all-gather.27.cloned.1.call-start
  11.3 28.0 %all-gather.17.cloned.1.call-done = f32[1024,256]{1,0:T(8,128)} async-done(((f32[256,256]{1,0:T(8,128)}), f32[1024,256]{1,0:T(8,128)}) %all-gather.17.cloned.1.call-update) | async-done | bytes 1048592 | tf_op jit(solution)/shard_map/all_gather | solution.py:31
  39.3 44.9 %all-gather.15.cloned.1.call-done = f32[1024,1024]{0,1:T(8,128)} async-done(((f32[1024,64]{0,1:T(8,128)}), f32[1024,1024]{0,1:T(8,128)}) %all-gather.15.cloned.1.call-update) | async-done | bytes 4194320 | tf_op jit(solution)/shard_map/all_gather | solution.py:39
  84.2 10.1 %fusion.12 = f32[1024,256]{1,0:T(8,128)} fusion(f32[1024,1024]{0,1:T(8,128)} %all-gather.15.cloned.1.call-done, f32[1024,256]{1,0:T(8,128)} %all-gather.17.cloned.1.call-done), kind=kOutput, calls=%fused_computation.36 | convolution fusion | flops 3221225472 | bytes 6291456 | tf_op jit(solution)/shard_map/dot_general | solution.py:38
  94.3 0.0 all-gather.27.cloned.1.call-update
  94.4 0.0 all-gather.19.cloned.1.call-start
  94.4 48.8 %all-gather.27.cloned.1.call-done = f32[4096,256]{1,0:T(8,128)} async-done(((f32[1024,256]{1,0:T(8,128)}), f32[4096,256]{1,0:T(8,128)}) %all-gather.27.cloned.1.call-update) | async-done | bytes 4194320 | tf_op jit(solution)/shard_map/all_gather | solution.py:26
  143.3 2.6 reduce_sum.54
  145.9 0.5 broadcast_select_fusion.1
  146.4 0.7 constant_dynamic-slice_fusion.3
  147.1 0.0 all-gather.19.cloned.1.call-update
  147.2 0.2 all-gather.29.cloned.1.call-start
  147.4 27.5 %all-gather.19.cloned.1.call-done = f32[1024,256]{1,0:T(8,128)} async-done(((f32[256,256]{1,0:T(8,128)}), f32[1024,256]{1,0:T(8,128)}) %all-gather.19.cloned.1.call-update) | async-done | bytes 1048592 | tf_op jit(solution)/shard_map/all_gather | solution.py:31
  174.9 10.1 %fusion.13 = f32[1024,256]{1,0:T(8,128)} fusion(f32[1024,1024]{0,1:T(8,128)} %all-gather.15.cloned.1.call-done, f32[1024,256]{1,0:T(8,128)} %all-gather.19.cloned.1.call-done), kind=kOutput, calls=%fused_computation.37 | convolution fusion | flops 3221225472 | bytes 6291456 | tf_op jit(solution)/shard_map/dot_general | solution.py:38
  185.0 0.0 all-gather.29.cloned.1.call-update
  185.0 0.0 all-gather.23.cloned.1.call-start
  185.1 50.6 %all-gather.29.cloned.1.call-done = f32[4096,256]{1,0:T(8,128)} async-done(((f32[1024,256]{1,0:T(8,128)}), f32[4096,256]{1,0:T(8,128)}) %all-gather.29.cloned.1.call-update) | async-done | bytes 4194320 | tf_op jit(solution)/shard_map/all_gather | solution.py:26
  235.7 2.6 reduce_sum.55
  238.3 0.2 multiply_subtract_fusion.1
  238.5 0.7 constant_dynamic-slice_fusion.1
  239.3 0.0 all-gather.23.cloned.1.call-update
  239.3 0.0 all-gather.21.cloned.1.call-start
  239.3 0.3 copy.5
  239.7 0.7 constant_dynamic-slice_fusion.2
  240.4 0.3 all-gather.31.cloned.1.call-start
  240.7 26.3 %all-gather.23.cloned.1.call-done = f32[1024,256]{1,0:T(8,128)} async-done(((f32[256,256]{1,0:T(8,128)}), f32[1024,256]{1,0:T(8,128)}) %all-gather.23.cloned.1.call-update) | async-done | bytes 1048592 | tf_op jit(solution)/shard_map/all_gather | solution.py:31
  267.0 44.9 %all-gather.21.cloned.1.call-done = f32[1024,1024]{0,1:T(8,128)} async-done(((f32[1024,64]{0,1:T(8,128)}), f32[1024,1024]{0,1:T(8,128)}) %all-gather.21.cloned.1.call-update) | async-done | bytes 4194320 | tf_op jit(solution)/shard_map/all_gather | solution.py:39
  311.9 10.1 %fusion.14 = f32[1024,256]{1,0:T(8,128)} fusion(f32[1024,1024]{0,1:T(8,128)} %all-gather.21.cloned.1.call-done, f32[1024,256]{1,0:T(8,128)} %all-gather.23.cloned.1.call-done), kind=kOutput, calls=%fused_computation.38 | convolution fusion | flops 3221225472 | bytes 6291456 | tf_op jit(solution)/shard_map/dot_general | solution.py:38
  322.0 0.0 all-gather.25.cloned.1.call-start
  322.1 48.9 %all-gather.31.cloned.1.call-done = f32[4096,256]{1,0:T(8,128)} async-done(((f32[1024,256]{1,0:T(8,128)}), f32[4096,256]{1,0:T(8,128)}) %all-gather.31.cloned.1.call-update) | async-done | bytes 4194320 | tf_op jit(solution)/shard_map/all_gather | solution.py:26
  370.9 2.6 reduce_sum.56
  373.5 0.1 broadcast_select_fusion
  373.6 0.7 constant_dynamic-slice_fusion
  374.4 0.3 all-gather.33.cloned.1.call-start
  374.7 27.4 %all-gather.25.cloned.1.call-done = f32[1024,256]{1,0:T(8,128)} async-done(((f32[256,256]{1,0:T(8,128)}), f32[1024,256]{1,0:T(8,128)}) %all-gather.25.cloned.1.call-update) | async-done | bytes 1048592 | tf_op jit(solution)/shard_map/all_gather | solution.py:31
  402.1 10.1 %fusion.15 = f32[1024,256]{1,0:T(8,128)} fusion(f32[1024,1024]{0,1:T(8,128)} %all-gather.21.cloned.1.call-done, f32[1024,256]{1,0:T(8,128)} %all-gather.25.cloned.1.call-done), kind=kOutput, calls=%fused_computation.39 | convolution fusion | flops 3221225472 | bytes 6291456 | tf_op jit(solution)/shard_map/dot_general | solution.py:38
  412.3 50.6 %all-gather.33.cloned.1.call-done = f32[4096,256]{1,0:T(8,128)} async-done(((f32[1024,256]{1,0:T(8,128)}), f32[4096,256]{1,0:T(8,128)}) %all-gather.33.cloned.1.call-update) | async-done | bytes 4194320 | tf_op jit(solution)/shard_map/all_gather | solution.py:26
  462.9 2.6 reduce_sum.57
  465.5 2.0 fusion
  467.4 129.7 %all-reduce = (f32[1]{0:T(128)}, f32[1]{0:T(128)}) all-reduce(f32[1]{0:T(128)} %bitcast.17, f32[1]{0:T(128)} %bitcast.16), channel_id=1, replica_groups=mesh['row'=4,'col'=16,'layer'=4] {'row','col'}, use_global_device_ids=true, to_apply=%region_7.8 | all-reduce | flops 2 | bytes 16 | tf_op jit(solution)/shard_map/psum | solution.py:75
  597.1 1.8 pad_maximum_fusion
  (10 shorter events, 0.1 us)
Async XLA Ops:
  7.2 32.2 %all-gather.17.cloned.1.call-start = ((), (), s32[]{:S(2)}) async-start(), calls=%async_computation.1 | async-start | bytes 1310720 | tf_op jit(solution)/shard_map/all_gather | solution.py:31
  8.9 75.3 %all-gather.15.cloned.1.call-start = ((), (), s32[]{:S(2)}) async-start(), calls=%async_computation | async-start | bytes 4456448 | tf_op jit(solution)/shard_map/all_gather | solution.py:39
  11.3 132.0 %all-gather.27.cloned.1.call-start = ((), (), s32[]{:S(2)}) async-start(), calls=%async_computation.6 | async-start | bytes 5242880 | tf_op jit(solution)/shard_map/all_gather | solution.py:26
  94.3 51.5 %copy-start = (s32[64,64]{1,0:T(8,128)S(1)}, s32[64,64]{1,0:T(8,128)}, u32[]{:S(2)}) copy-start(s32[64,64]{1,0:T(8,128)} %param.3) | copy-start | bytes 49156
  94.4 80.5 %all-gather.19.cloned.1.call-start = ((), (), s32[]{:S(2)}) async-start(), calls=%async_computation.2 | async-start | bytes 1310720 | tf_op jit(solution)/shard_map/all_gather | solution.py:31
  147.2 88.5 %all-gather.29.cloned.1.call-start = ((), (), s32[]{:S(2)}) async-start(), calls=%async_computation.7 | async-start | bytes 5242880 | tf_op jit(solution)/shard_map/all_gather | solution.py:26
  185.0 82.0 %all-gather.23.cloned.1.call-start = ((), (), s32[]{:S(2)}) async-start(), calls=%async_computation.4 | async-start | bytes 1310720 | tf_op jit(solution)/shard_map/all_gather | solution.py:31
  239.3 72.6 %all-gather.21.cloned.1.call-start = ((), (), s32[]{:S(2)}) async-start(), calls=%async_computation.3 | async-start | bytes 4456448 | tf_op jit(solution)/shard_map/all_gather | solution.py:39
  240.4 130.5 %all-gather.31.cloned.1.call-start = ((), (), s32[]{:S(2)}) async-start(), calls=%async_computation.8 | async-start | bytes 5242880 | tf_op jit(solution)/shard_map/all_gather | solution.py:26
  322.0 80.1 %all-gather.25.cloned.1.call-start = ((), (), s32[]{:S(2)}) async-start(), calls=%async_computation.5 | async-start | bytes 1310720 | tf_op jit(solution)/shard_map/all_gather | solution.py:31
  374.4 88.5 %all-gather.33.cloned.1.call-start = ((), (), s32[]{:S(2)}) async-start(), calls=%async_computation.9 | async-start | bytes 5242880 | tf_op jit(solution)/shard_map/all_gather | solution.py:26
Sparse Core Ops, SparseCore 0:
  9.8 29.4 all-gather.16
  41.7 42.4 all-gather.14
  94.5 48.7 all-gather.26
  147.3 27.5 all-gather.18
  185.1 50.4 all-gather.28
  239.4 27.5 all-gather.22
  269.4 42.4 all-gather.20
  322.1 48.7 all-gather.30
  374.5 27.5 all-gather.24
  412.4 50.4 all-gather.32
